TPU v7x, 512 devices: a whole 4x8x8 slice. The times are simulated.
512 devices in a mesh: band: 32 (over y, x_lo, core), tile: 16 (over x_hi, z).
Axes of the slice: x: 4 (x_hi: 2, x_lo: 2; x = x_hi * 2 + x_lo), y: 8, z: 8, core: 2. Of those that a mesh axis runs over, the one named last changes fastest.
Arguments:
- frames: bfloat16 [16384, 128], P('tile'), may hold values from -6 to 6
- projection: bfloat16 [8192, 128], replicated, may hold values from -0.0625 to 0.0625
- offsets: int32 [32, 8], P('band'), may hold values from 0 to 16383
Outputs:
- profile: float32 [32, 16384], P('band', 'tile')
All inputs are finite; a program needn't handle non-finite values.
Results may differ from a plain program's by a relative error of at most 0.0013.
Values may be sent and summed in bfloat16 or wider, within the bound.
A program may use at most 64 MiB of HBM per device.

v0:
```python
import math

import jax
import jax.numpy as jnp
from jax import lax
from jax.sharding import PartitionSpec as P

WIN = 64


def passed_along(value, axis, by):
    peers = lax.axis_size(axis)
    pairs = [(i, i + by) for i in range(peers) if 0 <= i + by < peers]
    return lax.ppermute(value, axis, pairs)


def make_sketch(extended, projection, count):
    width = math.gcd(count, 128)
    blocks = count // width
    channels = extended.shape[1]
    span = projection.shape[0] // channels

    def one_block(block):
        piece = lax.dynamic_slice_in_dim(extended, block * width, width + span - 1, 0)
        stacked = jnp.stack([piece[shift_k : shift_k + width] for shift_k in range(span)], axis=1)
        stacked = stacked.reshape(width, span * channels)
        return jnp.dot(stacked, projection, preferred_element_type=jnp.float32)

    values = lax.map(one_block, jnp.arange(blocks, dtype=jnp.int32))
    values = values.reshape(count, projection.shape[1])
    centred = values - jnp.mean(values, axis=1, keepdims=True)
    scaled = centred * lax.rsqrt(jnp.mean(centred * centred, axis=1, keepdims=True) + 1e-05)
    return scaled.astype(jnp.bfloat16)


def shards(frames, projection, offsets):
    rows = frames.shape[0]
    tile_count = lax.axis_size("tile")
    tile_pos = lax.axis_index("tile")
    total = rows * tile_count
    width_sk = projection.shape[1]
    following = passed_along(frames[: WIN - 1], "tile", -1)
    extended = jnp.concatenate([frames, following], axis=0)
    own_sketch = make_sketch(extended, projection, rows)
    sketches = lax.all_gather(own_sketch, "tile", axis=0, tiled=True)
    padded = jnp.concatenate([sketches, jnp.zeros((rows, width_sk), jnp.bfloat16)], axis=0)
    local_iota = jnp.arange(rows, dtype=jnp.int32)

    def one_offset(turn, best):
        offset = offsets[0, turn]
        row_start = tile_pos * rows
        col_start = row_start + offset

        def compute(best_now):
            row_block = lax.dynamic_slice_in_dim(sketches, row_start, rows, 0)
            col_block = lax.dynamic_slice_in_dim(padded, col_start, rows, 0)
            corr = (
                lax.dot_general(
                    row_block,
                    col_block,
                    (((1,), (1,)), ((), ())),
                    preferred_element_type=jnp.float32,
                )
                / width_sk
            )
            row_index = (row_start + local_iota)[:, None]
            col_index = (col_start + local_iota)[None, :]
            valid = (col_index < total) & (jnp.abs(row_index - col_index) >= WIN)
            masked = jnp.where(valid, corr, jnp.float32(-2.0))
            old_rows = lax.dynamic_slice_in_dim(best_now, row_start, rows, 0)
            best_now = lax.dynamic_update_slice_in_dim(
                best_now, jnp.maximum(old_rows, jnp.max(masked, axis=1)), row_start, 0
            )
            old_cols = lax.dynamic_slice_in_dim(best_now, col_start, rows, 0)
            return lax.dynamic_update_slice_in_dim(
                best_now, jnp.maximum(old_cols, jnp.max(masked, axis=0)), col_start, 0
            )

        def keep(best_now):
            return best_now

        return lax.cond(col_start < total, compute, keep, best)

    start_best = jnp.full((total + rows,), -2.0, jnp.float32)
    best = lax.fori_loop(0, offsets.shape[1], one_offset, start_best)
    trimmed = best[:total]
    merged = lax.pmax(trimmed, "tile")
    return lax.dynamic_slice_in_dim(merged, tile_pos * rows, rows, 0).reshape(1, rows)


def solution(mesh):
    in_specs = (P("tile", None), P(), P("band", None))
    out_specs = P("band", "tile")
    return jax.shard_map(shards, mesh=mesh, in_specs=in_specs, out_specs=out_specs, check_vma=False)
```

profile of v0, /device:TPU:1, one launch (start us, length us, event | category | flops | bytes accessed | tf_op | source)
XLA Modules:
  0.0 395.7 jit_solution(17560130912972209927)
XLA Ops:
  7.6 1.3 collective-permute-start
  9.0 4.8 %collective-permute-done = bf16[63,128]{0,1:T(8,128)(2,1)S(1)} collective-permute-done((bf16[63,128]{0,1:T(8,128)(2,1)S(1)}, bf16[63,128]{0,1:T(8,128)(2,1)S(1)}, u32[]{:S(2)}, u32[]{:S(2)}) %collective-permute-start) | collective-permute-done | bytes 16160 | tf_op jit(solution)/shard_map/ppermute | solution.py:14
  13.8 82.6 %while.30 = (s32[]{:T(128)}, f32[8,128,128]{2,1,0:T(8,128)S(1)}, s32[8]{0:T(128)S(1)}, bf16[1087,128]{0,1:T(8,128)(2,1)S(1)}, bf16[8192,128]{1,0:T(8,128)(2,1)},...) while((s32[]{:T(128)}, f32[8,128,128]{2,1,0:T(8,128)S(1)}, ...), condition=%wide.region_1.2_spmd, body=%wide.region_0.1_spmd.sunk | while | flops 268435520 | bytes 8455815 | solution.py:29
  21.8 2.3 fusion.20
  32.1 2.3 fusion.20
  42.5 2.3 fusion.20
  52.8 2.3 fusion.20
  63.1 2.3 fusion.20
  73.4 2.3 fusion.20
  83.8 2.3 fusion.20
  94.1 2.3 fusion.20
  98.2 110.3 %all-gather.2.cloned.1.call-done = bf16[16384,128]{1,0:T(8,128)(2,1)} async-done(((bf16[1024,128]{1,0:T(8,128)(2,1)}), bf16[16384,128]{1,0:T(8,128)(2,1)}) %all-gather.2.cloned.1.call-update) | async-done | bytes 4194320 | tf_op jit(solution)/shard_map/all_gather | solution.py:45
  208.5 5.1 %concatenate.7 = bf16[17408,128]{1,0:T(8,128)(2,1)} pad(bf16[16384,128]{1,0:T(8,128)(2,1)} %all-gather.2.cloned.1.call-done, bf16[]{:T(256)} %constant.94.clone.1), padding=0_1024x0_0 | pad | bytes 8650754 | tf_op jit(solution)/shard_map/concatenate | solution.py:46
  213.6 35.8 %while.31 = (s32[]{:T(128)}, f32[17408]{0:T(1024)S(1)}, s32[1,8]{1,0:T(1,128)S(1)}, s32[]{:T(128)}, bf16[16384,128]{1,0:T(8,128)(2,1)}, /*index=5*/bf16[17408,128]{1,0:T(8,128)(2,1)}, s32[]{:T(128)}, s32[]{:T(128)}) while((s32[]{:T(128)}, f32[17408]{0:T(1024)S(1)}, s32[1,8]{1,0:T(1,128)S(1)}, s32[]{:T(128)}, ...), condition=%wide.region_9.10_spmd.clone.clone, body=%wide.region_4.9_spmd.clone.clone.sunk | while | flops 276827136 | bytes 588080 | solution.py:85
  214.8 3.3 conditional.4
  214.8 2.9 fusion.4
  219.2 3.3 conditional.4
  219.3 2.9 fusion.4
  223.7 3.3 conditional.4
  223.7 2.9 fusion.4
  228.2 3.3 conditional.4
  228.2 2.9 fusion.4
  232.6 3.3 conditional.4
  232.7 2.9 fusion.4
  237.1 3.3 conditional.4
  237.2 2.9 fusion.4
  241.6 3.3 conditional.4
  241.6 2.9 fusion.4
  246.0 3.3 conditional.4
  246.1 2.9 fusion.4
  250.0 137.6 %all-reduce.3.cloned.1.call-done = f32[16384]{0:T(1024)} async-done(((f32[16384]{0:T(1024)}), f32[16384]{0:T(1024)}) %all-reduce.3.cloned.1.call-update) | async-done | bytes 65552 | tf_op jit(solution)/shard_map/pmax | solution.py:87
  387.6 1.3 dynamic_slice.31
  (586 shorter events, 66.9 us)
Async XLA Ops:
  6.5 201.9 %all-gather.2.cloned.1.call-start = ((), (), s32[]{:S(2)}) async-start(), calls=%async_computation | async-start | bytes 4456448 | tf_op jit(solution)/shard_map/all_gather | solution.py:45
  7.6 6.1 %collective-permute-start = (bf16[63,128]{0,1:T(8,128)(2,1)S(1)}, bf16[63,128]{0,1:T(8,128)(2,1)S(1)}, u32[]{:S(2)}, u32[]{:S(2)}) collective-permute-start(bf16[63,128]{0,1:T(8,128)(2,1)S(1)} %slice.200), channel_id=1, source_target_pairs={{1,0},{2,1},{3,2},{4,3},{5,4},{6,5},{7,6},{8,7},{9,8},{10,9},{11,1... | collective-permute-start | bytes 48392 | tf_op jit(solution)/shard_map/ppermute | solution.py:14
  98.1 289.5 %all-reduce.3.cloned.1.call-start = ((), (), s32[]{:S(2)}) async-start(), calls=%async_computation.1 | async-start | bytes 131072 | tf_op jit(solution)/shard_map/pmax | solution.py:87
  98.2 115.4 %copy-start = (s32[1,8]{1,0:T(1,128)S(1)}, s32[1,8]{1,0:T(1,128)}, u32[]{:S(2)}) copy-start(s32[1,8]{1,0:T(1,128)} %param.11) | copy-start | bytes 100
Sparse Core Ops, SparseCore 0:
  98.3 110.1 all-gather.1
  250.1 137.4 all-reduce.2
where the time goes:
time: 404 us; the launch traced here: 396 us
  waiting for transfers between devices  253 us (63%)
  local copies, waits for them, and re-layouts  68.6 us (17%)
  matrix products  42.3 us (10%)
  between operations  13.5 us (3%)
  loops' own time  12.8 us (3%)
  other arithmetic  4.6 us (1%)
    pmax x1, waiting for transfers between devices, shards(): merged = lax.pmax(trimmed, 'tile')  138 us
    all_gather x1, waiting for transfers between devices, shards(): sketches = lax.all_gather(own_sketch, 'tile', axis=0, tiled=True)  110 us
    while x504, local copies, waits for them, and re-layouts  50.5 us
    dot_general x8, matrix products, compute(): lax.dot_general(row_block, col_block, (((1,), (1,)), ((), ())), preferred...  23.5 us
    dot_general x8, matrix products, one_block(): return jnp.dot(stacked, projection, preferred_element_type=jnp.float32)  18.8 us
  transfers between devices with their start and end apart: 3, of which 3 were waited for; matrix products, arithmetic and copies ran while one was open for 0% of the time, Pallas kernels for 0%

commit v1 on v0

v1 whole, which is shorter than its diff:
```python
import functools

import jax
import jax.numpy as jnp
from jax import lax
from jax.experimental import pallas as pl
from jax.experimental.pallas import tpu as pltpu
from jax.sharding import PartitionSpec as P

MESH = pl.DeviceIdType.MESH
ROWS = 1024
HALF = 512
CH = 128
TAIL = 64
GROUP = 16
PIECES = 4
PIECE = HALF // PIECES
BANDS = 32
TILES = 16
NOFF = 8
LOW = -256.0


def pad_shift(value, by):
    return pltpu.roll(value, value.shape[0] - by, 0)


def sketch_rows(frames, proj):
    count = HALF + GROUP
    left = jnp.concatenate([frames[GROUP * a : GROUP * a + count] for a in range(4)], axis=1)

    def weights(c):
        return jnp.concatenate(
            [proj[(GROUP * a + c) * CH : (GROUP * a + c + 1) * CH, :] for a in range(4)], axis=0
        )

    def by_eight(c):
        right = jnp.concatenate([weights(c), weights(c + 8)], axis=1)
        both = jnp.dot(left, right, preferred_element_type=jnp.float32)
        return both[: HALF + 8, :CH] + both[8:, CH:]

    def by_four(c):
        return by_eight(c) + pad_shift(by_eight(c + 4), 4)

    def by_two(c):
        return by_four(c) + pad_shift(by_four(c + 2), 2)

    values = (by_two(0) + pad_shift(by_two(1), 1))[:HALF]
    centred = values - jnp.mean(values, axis=1, keepdims=True)
    scaled = centred * lax.rsqrt(jnp.mean(centred * centred, axis=1, keepdims=True) + 1e-05)
    return scaled.astype(jnp.bfloat16)


def corr_piece(piece, base, colsk, rowsk, xbuf):
    cols = colsk[PIECE * piece : PIECE * (piece + 1), :]
    apart = lax.broadcasted_iota(jnp.int32, (PIECE, 256), 1) - lax.broadcasted_iota(jnp.int32, (PIECE, 256), 0)
    for part in range(ROWS // 256):
        corr = lax.dot_general(
            cols,
            rowsk[256 * part : 256 * (part + 1), :],
            (((1,), (1,)), ((), ())),
            preferred_element_type=jnp.float32,
        )
        far = jnp.abs(apart + (base + 256 * part - PIECE * piece)) >= TAIL
        corr = jnp.where(far, corr, LOW)
        for side in range(2):
            xbuf[pl.ds(PIECE * piece * 8 + 2 * part + side, PIECE, stride=8), :] = corr[:, CH * side : CH * (side + 1)]


def column_of(xbuf, c):
    return xbuf[pl.ds(pl.multiple_of(c * 8, 8), 8), :]


def prefix_piece(piece, carry, xbuf, table):
    def step(c, best):
        best = jnp.maximum(best, column_of(xbuf, c))
        table[c + 1] = best
        return best

    return lax.fori_loop(PIECE * piece, PIECE * (piece + 1), step, carry, unroll=16)


def suffix_all(xbuf, table):
    low = jnp.full((8, CH), LOW, jnp.float32)
    table[2 * HALF] = low

    def step(k, best):
        c = HALF - 1 - k
        best = jnp.maximum(best, column_of(xbuf, c))
        table[HALF + c] = best
        return best

    lax.fori_loop(0, HALF, step, low, unroll=16)


def band_best(bb, isx, ksm, table, whole, place):
    best = jnp.full((8, CH), LOW, jnp.float32)
    for n in range(NOFF):
        best = jnp.maximum(best, table[isx[bb, n]])
        second = jnp.right_shift(place + ksm[bb, n], 10) == 0
        best = jnp.maximum(best, jnp.where(second, whole, LOW))
    return best * (1.0 / CH)


def kernel(
    frames, proj_hbm, offs, out, ext, proj, rowsk, colsk, xbuf, table, oall, ibuf, kbuf, isx, ksm, sbuf, rbuf,
    local_sem, tail_sem, offs_sem, half_sem, piece_send, piece_recv, out_sem,
):
    b, t = lax.axis_index("band"), lax.axis_index("tile")
    core, xl, y = lax.rem(b, 2), lax.rem(lax.div(b, 2), 2), lax.div(b, 4)
    xh, z = lax.div(t, 8), lax.rem(t, 8)
    partner = b + 1 - 2 * core
    chunk_block = xl * 8 + y
    base = (t - chunk_block) * ROWS - core * HALF

    load_frames = pltpu.make_async_copy(frames, ext.at[pl.ds(0, ROWS)], local_sem.at[0])
    load_frames.start()
    load_proj = pltpu.make_async_copy(proj_hbm, proj, local_sem.at[1])
    load_proj.start()

    def turned(step):
        return lax.rem(b + step, BANDS)

    def source(piece):
        ys = lax.rem(2 * piece + 1 - z - y + 16, 8)
        return (ys * 4 + (1 - xh) * 2 + core, xl * 8 + y)

    def target(piece):
        zt = lax.rem(2 * piece + 1 - z - y + 16, 8)
        return (z * 4 + xh * 2 + core, (1 - xl) * 8 + zt)

    barrier = pltpu.get_barrier_semaphore()

    def greet(step, carry):
        pl.semaphore_signal(barrier, inc=1, device_id=(turned(step), t), device_id_type=MESH)
        return carry

    pl.semaphore_signal(barrier, inc=1, device_id=(b, lax.rem(t + 1, TILES)), device_id_type=MESH)
    for piece in range(PIECES):
        pl.semaphore_signal(barrier, inc=1, device_id=source(piece), device_id_type=MESH)
    lax.fori_loop(1, BANDS, greet, 0)

    oall[pl.ds(b, 1), :] = jnp.zeros((1, CH), jnp.int32)
    oall[pl.ds(b, 1), 0:NOFF] = offs[...]
    pl.semaphore_wait(barrier, BANDS + PIECES)

    tail = pltpu.make_async_remote_copy(
        src_ref=frames.at[pl.ds(0, TAIL)],
        dst_ref=ext.at[pl.ds(ROWS, TAIL)],
        send_sem=tail_sem.at[0],
        recv_sem=tail_sem.at[1],
        device_id=(b, lax.rem(t + TILES - 1, TILES)),
        device_id_type=MESH,
    )
    tail.start()

    def offs_copy(rows, to):
        return pltpu.make_async_remote_copy(
            src_ref=oall.at[rows],
            dst_ref=oall.at[rows],
            send_sem=offs_sem.at[0],
            recv_sem=offs_sem.at[1],
            device_id=(to, t),
            device_id_type=MESH,
        )

    def send_offs(step, carry):
        offs_copy(pl.ds(b, 1), turned(step)).start()
        return carry

    lax.fori_loop(1, BANDS, send_offs, 0)

    load_frames.wait()
    load_proj.wait()
    tail.wait()

    @pl.when(t == TILES - 1)
    def _():
        ext[pl.ds(ROWS, TAIL), :] = jnp.zeros((TAIL, CH), jnp.bfloat16)

    mine = pl.ds(pl.multiple_of(core * HALF, HALF), HALF)
    rowsk[mine, :] = sketch_rows(ext[pl.ds(pl.multiple_of(core * HALF, HALF), HALF + TAIL), :], proj)

    half = pltpu.make_async_remote_copy(
        src_ref=rowsk.at[mine],
        dst_ref=rowsk.at[mine],
        send_sem=half_sem.at[0],
        recv_sem=half_sem.at[1],
        device_id=(partner, t),
        device_id_type=MESH,
    )
    pieces = [
        pltpu.make_async_remote_copy(
            src_ref=rowsk.at[pl.ds(pl.multiple_of(core * HALF + PIECE * piece, PIECE), PIECE)],
            dst_ref=colsk.at[pl.ds(PIECE * piece, PIECE)],
            send_sem=piece_send.at[piece],
            recv_sem=piece_recv.at[piece],
            device_id=target(piece),
            device_id_type=MESH,
        )
        for piece in range(PIECES)
    ]
    for copy in pieces:
        copy.start()
    half.start()

    offs_copy(pl.ds(0, BANDS - 1), b).wait()
    offsets = oall[...]
    reach = offsets + (base + ROWS)
    ibuf[...] = jnp.clip(reach, 0, HALF) + jnp.clip(reach - ROWS, 0, HALF)
    kbuf[...] = (t - chunk_block) * ROWS - offsets
    load_i = pltpu.make_async_copy(ibuf, isx, local_sem.at[2])
    load_k = pltpu.make_async_copy(kbuf, ksm, local_sem.at[3])
    load_i.start()
    load_k.start()
    half.wait_recv()

    low = jnp.full((8, CH), LOW, jnp.float32)
    table[0] = low
    whole = low
    for piece in range(PIECES):
        pieces[piece].wait_recv()
        corr_piece(piece, base, colsk, rowsk, xbuf)
        whole = prefix_piece(piece, whole, xbuf, table)
    suffix_all(xbuf, table)
    load_i.wait()
    load_k.wait()

    place = lax.broadcasted_iota(jnp.int32, (8, CH), 0) * CH + lax.broadcasted_iota(jnp.int32, (8, CH), 1)

    def out_copy(src, dst, to):
        return pltpu.make_async_remote_copy(
            src_ref=sbuf.at[src],
            dst_ref=rbuf.at[dst],
            send_sem=out_sem.at[0],
            recv_sem=out_sem.at[1],
            device_id=(to, t),
            device_id_type=MESH,
        )

    def send_best(step, carry):
        bb = turned(step)
        sbuf[bb] = band_best(bb, isx, ksm, table, whole, place)
        out_copy(pl.ds(bb, 1), pl.ds(b, 1), bb).start()
        return carry

    lax.fori_loop(1, BANDS, send_best, 0)
    rbuf[b] = band_best(b, isx, ksm, table, whole, place)

    every = out_copy(pl.ds(0, BANDS - 1), pl.ds(0, BANDS - 1), b)
    every.wait_recv()
    out[...] = jnp.max(rbuf[...], axis=0)
    every.wait_send()
    half.wait_send()
    for copy in pieces:
        copy.wait_send()


def shards(frames, projection, offsets):
    dma = pltpu.SemaphoreType.DMA
    best = pl.pallas_call(
        kernel,
        out_shape=jax.ShapeDtypeStruct((8, CH), jnp.float32),
        in_specs=[
            pl.BlockSpec(memory_space=pl.ANY),
            pl.BlockSpec(memory_space=pl.ANY),
            pl.BlockSpec(memory_space=pltpu.VMEM),
        ],
        out_specs=pl.BlockSpec(memory_space=pltpu.VMEM),
        scratch_shapes=[
            pltpu.VMEM((ROWS + TAIL, CH), jnp.bfloat16),
            pltpu.VMEM((TAIL * CH, CH), jnp.bfloat16),
            pltpu.VMEM((ROWS, CH), jnp.bfloat16),
            pltpu.VMEM((HALF, CH), jnp.bfloat16),
            pltpu.VMEM((HALF * 8, CH), jnp.float32),
            pltpu.VMEM((2 * HALF + 1, 8, CH), jnp.float32),
            pltpu.VMEM((BANDS, CH), jnp.int32),
            pltpu.VMEM((BANDS, CH), jnp.int32),
            pltpu.VMEM((BANDS, CH), jnp.int32),
            pltpu.SMEM((BANDS, CH), jnp.int32),
            pltpu.SMEM((BANDS, CH), jnp.int32),
            pltpu.VMEM((BANDS, 8, CH), jnp.float32),
            pltpu.VMEM((BANDS, 8, CH), jnp.float32),
            dma((4,)),
            dma((2,)),
            dma((2,)),
            dma((2,)),
            dma((PIECES,)),
            dma((PIECES,)),
            dma((2,)),
        ],
        compiler_params=pltpu.CompilerParams(
            collective_id=0, has_side_effects=True, vmem_limit_bytes=48 * 1024 * 1024
        ),
    )(frames, projection, offsets)
    return best.reshape(1, ROWS)


def solution(mesh):
    in_specs = (P("tile", None), P(), P("band", None))
    out_specs = P("band", "tile")
    return jax.shard_map(shards, mesh=mesh, in_specs=in_specs, out_specs=out_specs, check_vma=False)
```

time: 404 us -> 49.5 us (0.12); the launches traced: 396 us -> 49.3 us
  waiting for transfers between devices: 253 us -> 0 us
  local copies, waits for them, and re-layouts: 68.6 us -> 3.79 us
  Pallas kernels: 0 us -> 45.5 us
  matrix products: 42.3 us -> 0 us
  between operations: 13.5 us -> 0.01 us
  loops' own time: 12.8 us -> 0 us
  other arithmetic: 4.6 us -> 0 us
    pmax x1 -> x0, waiting for transfers between devices: 138 us -> none  [shards(): merged = lax.pmax(trimmed, 'tile')]
    all_gather x1 -> x0, waiting for transfers between devices: 110 us -> none  [shards(): sketches = lax.all_gather(own_sketch, 'tile', axis=0, tiled=True)]
    while x504 -> x0, local copies, waits for them, and re-layouts: 50.5 us -> none
    pallas_call x0 -> x1, Pallas kernels: none -> 45.5 us  [shards(): pl.pallas_call(kernel, out_shape=jax.ShapeDtypeStruct((8, CH), jnp.float3...]
    dot_general x16 -> x0, matrix products: 42.3 us -> none  [the longest x8 23.5 us: compute(): lax.dot_general(row_block, col_block, (((1,), (1,)), ((), ())), preferred...]
    another operation x10 -> x0, loops' own time: 12.8 us -> none  [the longest x1 7.89 us: make_sketch(): values = lax.map(one_block, jnp.arange(blocks, dtype=jnp.int32))]
    dynamic_slice x17 -> x0, local copies, waits for them, and re-layouts: 10.3 us -> none  [the longest x8 4.66 us: make_sketch(): values = lax.map(one_block, jnp.arange(blocks, dtype=jnp.int32))]
    concatenate x1 -> x0, local copies, waits for them, and re-layouts: 5.15 us -> none  [shards(): jnp.concatenate([sketches, jnp.zeros((rows, width_sk), jnp.bfloat16)], ax...]
  transfers between devices with their start and end apart: 3 -> 0, of which waited for: 3 -> 0; matrix products, arithmetic and copies ran while one was open for 0% -> 0% of each run, Pallas kernels for 0% -> 0%
where the time goes in v1:
time: 49.5 us; the launch traced here: 49.3 us
  Pallas kernels  45.5 us (92%)
  local copies, waits for them, and re-layouts  3.79 us (8%)
    pallas_call x1, Pallas kernels, shards(): pl.pallas_call(kernel, out_shape=jax.ShapeDtypeStruct((8, CH), jnp.float3...  45.5 us
    unnamed x7, local copies, waits for them, and re-layouts  3.79 us

profile of v1, /device:TPU:1, one launch (start us, length us, event | category | flops | bytes accessed | tf_op | source)
XLA Modules:
  0.0 49.3 jit_solution(10573973144570555850)
XLA Ops:
  0.0 0.0 copy-start
  0.0 1.6 %copy-done = bf16[8192,128]{1,0:T(8,128)(2,1)S(1)} copy-done((bf16[8192,128]{1,0:T(8,128)(2,1)S(1)}, bf16[8192,128]{1,0:T(8,128)(2,1)}, u32[]{:S(2)}) %copy-start) | copy-done | bytes 2097176
  1.6 0.0 copy-start.1
  1.6 0.9 %copy-done.1 = bf16[1024,128]{1,0:T(8,128)(2,1)S(1)} copy-done((bf16[1024,128]{1,0:T(8,128)(2,1)S(1)}, bf16[1024,128]{1,0:T(8,128)(2,1)}, u32[]{:S(2)}) %copy-start.1) | copy-done | bytes 262168
  2.5 0.0 copy-start.2
  2.5 0.7 %copy-done.2 = s32[1,8]{1,0:T(1,128)S(1)} copy-done((s32[1,8]{1,0:T(1,128)S(1)}, s32[1,8]{1,0:T(1,128)}, u32[]{:S(2)}) %copy-start.2) | copy-done | bytes 56
  3.2 45.5 %shard_map.37 = f32[8,128]{1,0:T(8,128)S(1)} custom-call(bf16[1024,128]{1,0:T(8,128)(2,1)S(1)} %copy-done.1, bf16[8192,128]{1,0:T(8,128)(2,1)S(1)} %copy-done, s32[1,8]{1,0:T(1,128)S(1)} %copy-done.2), custom_call_target="tpu_custom_call" | custom-call | tf_op jit(solution)/shard_map/pallas_call | solution.py:261
  48.7 0.6 %copy.5 = f32[1,1024]{1,0:T(1,128)} copy(f32[1,1024]{1,0:T(1,128)S(1)} %bitcast.1) | data formatting | bytes 8192
Async XLA Ops:
  0.0 1.6 %copy-start = (bf16[8192,128]{1,0:T(8,128)(2,1)S(1)}, bf16[8192,128]{1,0:T(8,128)(2,1)}, u32[]{:S(2)}) copy-start(bf16[8192,128]{1,0:T(8,128)(2,1)} %proj_hbm.1) | copy-start | bytes 6291460
  1.6 0.9 %copy-start.1 = (bf16[1024,128]{1,0:T(8,128)(2,1)S(1)}, bf16[1024,128]{1,0:T(8,128)(2,1)}, u32[]{:S(2)}) copy-start(bf16[1024,128]{1,0:T(8,128)(2,1)} %frames.1) | copy-start | bytes 786436
  2.5 0.7 %copy-start.2 = (s32[1,8]{1,0:T(1,128)S(1)}, s32[1,8]{1,0:T(1,128)}, u32[]{:S(2)}) copy-start(s32[1,8]{1,0:T(1,128)} %offs.1) | copy-start | bytes 100

commit v2 on v1

v2 whole, which is shorter than its diff:
```python
import functools

import jax
import jax.numpy as jnp
from jax import lax
from jax.experimental import pallas as pl
from jax.experimental.pallas import tpu as pltpu
from jax.sharding import PartitionSpec as P

MESH = pl.DeviceIdType.MESH
ROWS = 1024
HALF = 512
CH = 128
TAIL = 64
GROUP = 16
PIECES = 4
PIECE = HALF // PIECES
BANDS = 32
CHIPS = 16
TILES = 16
NOFF = 8
LOW = -256.0


def pad_shift(value, by):
    return pltpu.roll(value, value.shape[0] - by, 0)


def sketch_rows(frames, proj):
    count = HALF + GROUP
    left = jnp.concatenate([frames[GROUP * a : GROUP * a + count] for a in range(4)], axis=1)

    def weights(c):
        return jnp.concatenate(
            [proj[(GROUP * a + c) * CH : (GROUP * a + c + 1) * CH, :] for a in range(4)], axis=0
        )

    def by_eight(c):
        right = jnp.concatenate([weights(c), weights(c + 8)], axis=1)
        both = jnp.dot(left, right, preferred_element_type=jnp.float32)
        return both[: HALF + 8, :CH] + both[8:, CH:]

    def by_four(c):
        return by_eight(c) + pad_shift(by_eight(c + 4), 4)

    def by_two(c):
        return by_four(c) + pad_shift(by_four(c + 2), 2)

    values = (by_two(0) + pad_shift(by_two(1), 1))[:HALF]
    centred = values - jnp.mean(values, axis=1, keepdims=True)
    scaled = centred * lax.rsqrt(jnp.mean(centred * centred, axis=1, keepdims=True) + 1e-05)
    return scaled.astype(jnp.bfloat16)


def corr_piece(piece, base, colsk, rowsk, xbuf):
    cols = colsk[PIECE * piece : PIECE * (piece + 1), :]
    apart = lax.broadcasted_iota(jnp.int32, (PIECE, 256), 1) - lax.broadcasted_iota(jnp.int32, (PIECE, 256), 0)
    for part in range(ROWS // 256):
        corr = lax.dot_general(
            cols,
            rowsk[256 * part : 256 * (part + 1), :],
            (((1,), (1,)), ((), ())),
            preferred_element_type=jnp.float32,
        )
        far = jnp.abs(apart + (base + 256 * part - PIECE * piece)) >= TAIL
        corr = jnp.where(far, corr, LOW)
        for side in range(2):
            xbuf[pl.ds(PIECE * piece * 8 + 2 * part + side, PIECE, stride=8), :] = corr[:, CH * side : CH * (side + 1)]


def column_of(xbuf, c):
    return xbuf[pl.ds(pl.multiple_of(c * 8, 8), 8), :]


def prefix_piece(piece, carry, xbuf, table):
    def step(c, best):
        best = jnp.maximum(best, column_of(xbuf, c))
        table[c + 1] = best
        return best

    return lax.fori_loop(PIECE * piece, PIECE * (piece + 1), step, carry, unroll=16)


def suffix_all(xbuf, table):
    low = jnp.full((8, CH), LOW, jnp.float32)
    table[2 * HALF] = low

    def step(k, best):
        c = HALF - 1 - k
        best = jnp.maximum(best, column_of(xbuf, c))
        table[HALF + c] = best
        return best

    lax.fori_loop(0, HALF, step, low, unroll=16)


def band_best(band, isx, ksm, table, whole, place):
    best = jnp.full((8, CH), LOW, jnp.float32)
    for n in range(NOFF):
        best = jnp.maximum(best, table[isx[band, n]])
        second = jnp.right_shift(place + ksm[band, n], 10) == 0
        best = jnp.maximum(best, jnp.where(second, whole, LOW))
    return best * (1.0 / CH)


def kernel(
    frames, proj_hbm, offs, out, ext, cext, proj, rowsk, colsk, xbuf, table, oall, ibuf, kbuf, isx, ksm, sbuf, rbuf,
    fin, other, local_sem, tail_sem, cols_send, cols_recv, offs_send, offs_recv, out_sem, fin_sem,
):
    b, t = lax.axis_index("band"), lax.axis_index("tile")
    core, xl, y = lax.rem(b, 2), lax.rem(lax.div(b, 2), 2), lax.div(b, 4)
    xh, z = lax.div(t, 8), lax.rem(t, 8)
    chip = lax.div(b, 2)
    zs = jnp.where(y < 4, 7 - 2 * y, 2 * y - 8)
    chunk_block = xl * 8 + zs
    base = (t - chunk_block) * ROWS - core * HALF
    partner = (b + 1 - 2 * core, t)
    beside = (b + 2 - 4 * xl, t)
    up = (lax.rem(b + 4, BANDS), t)
    down = (lax.rem(b + BANDS - 4, BANDS), t)
    is_source = z == zs
    on_diagonal = xl == xh
    is_own = jnp.logical_and(is_source, on_diagonal)
    swapped = y * 4 + xh * 2 + core

    def remote(src, dst, send_sem, recv_sem, to):
        return pltpu.make_async_remote_copy(
            src_ref=src, dst_ref=dst, send_sem=send_sem, recv_sem=recv_sem, device_id=to, device_id_type=MESH
        )

    load_frames = pltpu.make_async_copy(frames, ext.at[pl.ds(0, ROWS)], local_sem.at[0])
    load_frames.start()
    load_proj = pltpu.make_async_copy(proj_hbm, proj, local_sem.at[1])
    load_proj.start()

    barrier = pltpu.get_barrier_semaphore()

    @pl.when(jnp.logical_not(is_own))
    def _():
        pl.semaphore_signal(barrier, inc=1, device_id=(swapped, chunk_block), device_id_type=MESH)

    for peer in ((b, lax.rem(t + 1, TILES)), up, down, beside, partner):
        pl.semaphore_signal(barrier, inc=1, device_id=peer, device_id_type=MESH)

    oall[pl.ds(b, 1), :] = jnp.zeros((1, CH), jnp.int32)
    oall[pl.ds(b, 1), 0:NOFF] = offs[...]
    targets = jnp.where(is_source, jnp.where(on_diagonal, 7, 8), 0)
    pl.semaphore_wait(barrier, 5 + targets)

    tail = remote(
        frames.at[pl.ds(0, TAIL)], ext.at[pl.ds(ROWS, TAIL)], tail_sem.at[0], tail_sem.at[1],
        (b, lax.rem(t + TILES - 1, TILES)),
    )
    tail.start()

    def offs_copy(rows, at, to):
        return remote(oall.at[rows], oall.at[rows], offs_send.at[at], offs_recv.at[at], to)

    def row_of(behind):
        return pl.ds(lax.rem(y + behind + 8, 8) * 4, 4)

    to_partner = offs_copy(pl.ds(b, 1), 0, partner)
    to_beside = offs_copy(pl.ds(chip * 2, 2), 1, beside)
    rise = [offs_copy(row_of(-k), 2 + k, up) for k in range(4)]
    fall = [offs_copy(row_of(k), 6 + k, down) for k in range(3)]
    to_partner.start()

    load_frames.wait()
    tail.wait_recv()

    @pl.when(t == TILES - 1)
    def _():
        ext[pl.ds(ROWS, TAIL), :] = jnp.zeros((TAIL, CH), jnp.bfloat16)

    part = pl.ds(pl.multiple_of(core * HALF, HALF), HALF + TAIL)

    def cols_copy(zt):
        return remote(ext.at[part], cext, cols_send.at[zt], cols_recv.at[0], (swapped, xl * 8 + zt))

    cols_own = pltpu.make_async_copy(ext.at[part], cext, cols_recv.at[0])
    for zt in range(8):
        own = jnp.logical_and(is_own, z == zt)

        @pl.when(jnp.logical_and(is_source, jnp.logical_not(own)))
        def _():
            cols_copy(zt).start()

        @pl.when(own)
        def _():
            cols_own.start()

    to_partner.wait_recv()
    to_beside.start()
    load_proj.wait()
    rowsk[0:HALF, :] = sketch_rows(ext[0 : HALF + TAIL, :], proj)
    to_beside.wait_recv()
    rise[0].start()
    fall[0].start()
    rowsk[HALF:ROWS, :] = sketch_rows(ext[HALF : ROWS + TAIL, :], proj)
    for k in range(4):
        rise[k].wait_recv()
        if k < 3:
            rise[k + 1].start()
            fall[k].wait_recv()
        if k < 2:
            fall[k + 1].start()

    offsets = oall[...]
    reach = offsets + (base + ROWS)
    ibuf[...] = jnp.clip(reach, 0, HALF) + jnp.clip(reach - ROWS, 0, HALF)
    kbuf[...] = (t - chunk_block) * ROWS - offsets
    load_i = pltpu.make_async_copy(ibuf, isx, local_sem.at[2])
    load_k = pltpu.make_async_copy(kbuf, ksm, local_sem.at[3])
    load_i.start()
    load_k.start()

    cols_own.wait()
    colsk[...] = sketch_rows(cext[...], proj)

    low = jnp.full((8, CH), LOW, jnp.float32)
    table[0] = low
    whole = low
    for piece in range(PIECES):
        corr_piece(piece, base, colsk, rowsk, xbuf)
        whole = prefix_piece(piece, whole, xbuf, table)
    suffix_all(xbuf, table)
    load_i.wait()
    load_k.wait()

    place = lax.broadcasted_iota(jnp.int32, (8, CH), 0) * CH + lax.broadcasted_iota(jnp.int32, (8, CH), 1)

    def out_copy(src, dst, to):
        return remote(sbuf.at[src], rbuf.at[dst], out_sem.at[0], out_sem.at[1], (to * 2 + core, t))

    def send_best(k, carry):
        step = 8 + jnp.where(lax.rem(k, 2) == 1, lax.div(k + 1, 2), -lax.div(k, 2))
        to = lax.rem(chip + step, CHIPS)
        for side in range(2):
            sbuf[to, side] = band_best(to * 2 + side, isx, ksm, table, whole, place)
        out_copy(pl.ds(to, 1), pl.ds(chip, 1), to).start()
        return carry

    lax.fori_loop(0, CHIPS - 1, send_best, 0)
    for side in range(2):
        rbuf[chip, side] = band_best(chip * 2 + side, isx, ksm, table, whole, place)

    every = out_copy(pl.ds(0, CHIPS - 1), pl.ds(0, CHIPS - 1), chip)
    every.wait_recv()
    fin[...] = jnp.max(rbuf[...], axis=0)
    swap = remote(fin.at[pl.ds(1 - core, 1)], other, fin_sem.at[0], fin_sem.at[1], partner)
    swap.start()
    swap.wait_recv()
    best = jnp.maximum(fin[core], other[0])
    for group in range(8):
        out[:, CH * group : CH * (group + 1)] = best[group : group + 1, :]

    swap.wait_send()
    every.wait_send()
    tail.wait_send()
    to_partner.wait_send()
    to_beside.wait_send()
    for copy in rise + fall:
        copy.wait_send()
    for zt in range(8):

        @pl.when(jnp.logical_and(is_source, jnp.logical_not(jnp.logical_and(is_own, z == zt))))
        def _():
            cols_copy(zt).wait_send()


def shards(frames, projection, offsets):
    dma = pltpu.SemaphoreType.DMA
    return pl.pallas_call(
        kernel,
        out_shape=jax.ShapeDtypeStruct((1, ROWS), jnp.float32),
        in_specs=[
            pl.BlockSpec(memory_space=pl.ANY),
            pl.BlockSpec(memory_space=pl.ANY),
            pl.BlockSpec(memory_space=pltpu.VMEM),
        ],
        out_specs=pl.BlockSpec(memory_space=pltpu.VMEM),
        scratch_shapes=[
            pltpu.VMEM((ROWS + TAIL, CH), jnp.bfloat16),
            pltpu.VMEM((HALF + TAIL, CH), jnp.bfloat16),
            pltpu.VMEM((TAIL * CH, CH), jnp.bfloat16),
            pltpu.VMEM((ROWS, CH), jnp.bfloat16),
            pltpu.VMEM((HALF, CH), jnp.bfloat16),
            pltpu.VMEM((HALF * 8, CH), jnp.float32),
            pltpu.VMEM((2 * HALF + 1, 8, CH), jnp.float32),
            pltpu.VMEM((BANDS, CH), jnp.int32),
            pltpu.VMEM((BANDS, CH), jnp.int32),
            pltpu.VMEM((BANDS, CH), jnp.int32),
            pltpu.SMEM((BANDS, CH), jnp.int32),
            pltpu.SMEM((BANDS, CH), jnp.int32),
            pltpu.VMEM((CHIPS, 2, 8, CH), jnp.float32),
            pltpu.VMEM((CHIPS, 2, 8, CH), jnp.float32),
            pltpu.VMEM((2, 8, CH), jnp.float32),
            pltpu.VMEM((1, 8, CH), jnp.float32),
            dma((4,)),
            dma((2,)),
            dma((8,)),
            dma((1,)),
            dma((9,)),
            dma((9,)),
            dma((2,)),
            dma((2,)),
        ],
        compiler_params=pltpu.CompilerParams(
            collective_id=0, has_side_effects=True, vmem_limit_bytes=62 * 1024 * 1024
        ),
    )(frames, projection, offsets)


def solution(mesh):
    in_specs = (P("tile", None), P(), P("band", None))
    out_specs = P("band", "tile")
    return jax.shard_map(shards, mesh=mesh, in_specs=in_specs, out_specs=out_specs, check_vma=False)
```

time: 49.5 us -> 43.1 us (0.87)
  Pallas kernels: 45.5 us -> 41.7 us
  local copies, waits for them, and re-layouts: 3.79 us -> 1.28 us
    pallas_call x1, Pallas kernels: 45.5 us -> 41.7 us  [shards(): pl.pallas_call(kernel, out_shape=jax.ShapeDtypeStruct((1, ROWS), jnp.floa...]
    unnamed x7 -> x1, local copies, waits for them, and re-layouts: 3.79 us -> 1.28 us
where the time goes in v2:
time: 43.1 us; the launch traced here: 43 us
  Pallas kernels  41.7 us (97%)
  local copies, waits for them, and re-layouts  1.28 us (3%)
    pallas_call x1, Pallas kernels, shards(): pl.pallas_call(kernel, out_shape=jax.ShapeDtypeStruct((1, ROWS), jnp.floa...  41.7 us
    unnamed x1, local copies, waits for them, and re-layouts  1.28 us

profile of v2, /device:TPU:1, one launch (start us, length us, event | category | flops | bytes accessed | tf_op | source)
XLA Modules:
  0.0 43.0 jit_solution(4791803403100348814)
XLA Ops:
  0.0 41.7 %shard_map.37 = f32[1,1024]{1,0:T(1,128)} custom-call(bf16[1024,128]{1,0:T(8,128)(2,1)} %frames.1, bf16[8192,128]{1,0:T(8,128)(2,1)} %proj_hbm.1, s32[1,8]{1,0:T(1,128)} %offs.1), custom_call_target="tpu_custom_call" | custom-call | tf_op jit(solution)/shard_map/pallas_call | solution.py:273
  41.7 1.3 %copy.5 = f32[1,1024]{1,0:T(1,128)} copy(f32[1,1024]{1,0:T(1,128)} %shard_map.37) | data formatting | bytes 8192

commit v3 on v2

--- a/solution.py
+++ b/solution.py
@@ -72,26 +72,22 @@
     return xbuf[pl.ds(pl.multiple_of(c * 8, 8), 8), :]
 
 
-def prefix_piece(piece, carry, xbuf, table):
-    def step(c, best):
-        best = jnp.maximum(best, column_of(xbuf, c))
-        table[c + 1] = best
-        return best
-
-    return lax.fori_loop(PIECE * piece, PIECE * (piece + 1), step, carry, unroll=16)
-
-
-def suffix_all(xbuf, table):
+def running_best(xbuf, table):
     low = jnp.full((8, CH), LOW, jnp.float32)
+    table[0] = low
     table[2 * HALF] = low
 
-    def step(k, best):
-        c = HALF - 1 - k
-        best = jnp.maximum(best, column_of(xbuf, c))
-        table[HALF + c] = best
-        return best
-
-    lax.fori_loop(0, HALF, step, low, unroll=16)
+    def step(c, carry):
+        first, last = carry
+        first = jnp.maximum(first, column_of(xbuf, c))
+        table[c + 1] = first
+        d = HALF - 1 - c
+        last = jnp.maximum(last, column_of(xbuf, d))
+        table[HALF + d] = last
+
+        return first, last
+
+    return lax.fori_loop(0, HALF, step, (low, low), unroll=16)[0]
 
 
 def band_best(band, isx, ksm, table, whole, place):
@@ -104,24 +100,26 @@
 
 
 def kernel(
-    frames, proj_hbm, offs, out, ext, cext, proj, rowsk, colsk, xbuf, table, oall, ibuf, kbuf, isx, ksm, sbuf, rbuf,
-    fin, other, local_sem, tail_sem, cols_send, cols_recv, offs_send, offs_recv, out_sem, fin_sem,
+    frames, proj_hbm, offs_hbm, out, offs, ext, cext, proj, rowsk, colsk, xbuf, table, oall, ibuf, kbuf, isx, ksm, sbuf, rbuf,
+    fin, other, local_sem, tail_sem, pass_send, cols_send, next_send, cols_recv, offs_send, offs_recv, out_sem, fin_sem,
 ):
     b, t = lax.axis_index("band"), lax.axis_index("tile")
     core, xl, y = lax.rem(b, 2), lax.rem(lax.div(b, 2), 2), lax.div(b, 4)
     xh, z = lax.div(t, 8), lax.rem(t, 8)
     chip = lax.div(b, 2)
-    zs = jnp.where(y < 4, 7 - 2 * y, 2 * y - 8)
+    zs = lax.rem(jnp.where(y < 4, 2 * y, 15 - 2 * y) + 4 * core, 8)
     chunk_block = xl * 8 + zs
     base = (t - chunk_block) * ROWS - core * HALF
     partner = (b + 1 - 2 * core, t)
-    beside = (b + 2 - 4 * xl, t)
-    up = (lax.rem(b + 4, BANDS), t)
-    down = (lax.rem(b + BANDS - 4, BANDS), t)
+    after, before = lax.rem(t + 1, TILES), lax.rem(t + TILES - 1, TILES)
     is_source = z == zs
-    on_diagonal = xl == xh
-    is_own = jnp.logical_and(is_source, on_diagonal)
+    is_next = jnp.logical_and(lax.rem(before, 8) == zs, core == 1)
+    source_own = jnp.logical_and(is_source, xl == xh)
+    next_own = jnp.logical_and(t == lax.rem(chunk_block + 1, TILES), jnp.logical_and(xl == xh, core == 1))
+    next_on_line = lax.div(before, 8) == xl
     swapped = y * 4 + xh * 2 + core
+    gets_tail = jnp.logical_or(z != 7, y == 0)
+    gives_tail = jnp.logical_or(z != 0, y == 0)
 
     def remote(src, dst, send_sem, recv_sem, to):
         return pltpu.make_async_remote_copy(
@@ -129,81 +127,152 @@
         )
 
     load_frames = pltpu.make_async_copy(frames, ext.at[pl.ds(0, ROWS)], local_sem.at[0])
+    load_offs = pltpu.make_async_copy(offs_hbm, offs, local_sem.at[4])
+    load_offs.start()
     load_frames.start()
     load_proj = pltpu.make_async_copy(proj_hbm, proj, local_sem.at[1])
     load_proj.start()
 
     barrier = pltpu.get_barrier_semaphore()
 
-    @pl.when(jnp.logical_not(is_own))
-    def _():
-        pl.semaphore_signal(barrier, inc=1, device_id=(swapped, chunk_block), device_id_type=MESH)
-
-    for peer in ((b, lax.rem(t + 1, TILES)), up, down, beside, partner):
-        pl.semaphore_signal(barrier, inc=1, device_id=peer, device_id_type=MESH)
+    def greet(to):
+        pl.semaphore_signal(barrier, inc=1, device_id=to, device_id_type=MESH)
+
+    def along(step):
+        return (lax.rem(chip + step, CHIPS) * 2 + core, t)
+
+    @pl.when(jnp.logical_not(source_own))
+    def _():
+        greet((swapped, chunk_block))
+
+    @pl.when(jnp.logical_and(core == 1, jnp.logical_not(next_own)))
+    def _():
+        greet((swapped, lax.rem(chunk_block + 1, TILES)))
+
+    @pl.when(gets_tail)
+    def _():
+        greet((b, after))
+
+    greet(partner)
+
+    def greet_chip(step, carry):
+        greet(along(step))
+        return carry
+
+    lax.fori_loop(1, CHIPS, greet_chip, 0)
 
     oall[pl.ds(b, 1), :] = jnp.zeros((1, CH), jnp.int32)
+    load_offs.wait()
     oall[pl.ds(b, 1), 0:NOFF] = offs[...]
-    targets = jnp.where(is_source, jnp.where(on_diagonal, 7, 8), 0)
-    pl.semaphore_wait(barrier, 5 + targets)
-
-    tail = remote(
-        frames.at[pl.ds(0, TAIL)], ext.at[pl.ds(ROWS, TAIL)], tail_sem.at[0], tail_sem.at[1],
-        (b, lax.rem(t + TILES - 1, TILES)),
+    as_source = jnp.where(is_source, jnp.where(xl == xh, 7, 8), 0)
+    as_next = jnp.where(is_next, jnp.where(jnp.logical_and(next_on_line, xl == xh), 7, 8), 0)
+    pl.semaphore_wait(barrier, CHIPS + as_source + as_next + jnp.where(gives_tail, 1, 0))
+
+    tail_at = ext.at[pl.ds(ROWS, TAIL)]
+    tail = remote(frames.at[pl.ds(0, TAIL)], tail_at, tail_sem.at[0], tail_sem.at[1], (b, before))
+
+    @pl.when(gives_tail)
+    def _():
+        tail.start()
+
+    def cols_copy(zt, rows):
+        part = pl.ds(pl.multiple_of(core * HALF, HALF), rows)
+        return remote(
+            frames.at[part], cext.at[pl.ds(0, rows)], cols_send.at[zt], cols_recv.at[0], (swapped, xl * 8 + zt)
+        )
+
+    def cols_own(rows):
+        part = pl.ds(pl.multiple_of(core * HALF, HALF), rows)
+        return pltpu.make_async_copy(frames.at[part], cext.at[pl.ds(0, rows)], cols_recv.at[0])
+
+    def next_copy(zt):
+        to = (y * 4 + lax.div(before, 8) * 2 + core, xl * 8 + zt)
+        return remote(frames.at[pl.ds(0, TAIL)], cext.at[pl.ds(HALF, TAIL)], next_send.at[zt], cols_recv.at[1], to)
+
+    next_copy_own = pltpu.make_async_copy(frames.at[pl.ds(0, TAIL)], cext.at[pl.ds(HALF, TAIL)], cols_recv.at[1])
+
+    def sized(what):
+        @pl.when(core == 0)
+        def _():
+            what(HALF + TAIL)
+
+        @pl.when(core == 1)
+        def _():
+            what(HALF)
+
+    def each_target(cols_do, next_do, cols_do_own, next_do_own):
+        @pl.when(is_source)
+        def _():
+            for zt in range(8):
+                own = jnp.logical_and(source_own, z == zt)
+
+                @pl.when(jnp.logical_not(own))
+                def _():
+                    sized(functools.partial(cols_do, zt))
+
+                if cols_do_own is not None:
+
+                    @pl.when(own)
+                    def _():
+                        sized(cols_do_own)
+
+        @pl.when(is_next)
+        def _():
+            for zt in range(8):
+                own = jnp.logical_and(next_own, z == zt)
+
+                @pl.when(jnp.logical_not(own))
+                def _():
+                    next_do(zt)
+
+                if next_do_own is not None:
+
+                    @pl.when(own)
+                    def _():
+                        next_do_own()
+
+    each_target(
+        lambda zt, rows: cols_copy(zt, rows).start(),
+        lambda zt: next_copy(zt).start(),
+        lambda rows: cols_own(rows).start(),
+        lambda: next_copy_own.start(),
     )
-    tail.start()
 
     def offs_copy(rows, at, to):
         return remote(oall.at[rows], oall.at[rows], offs_send.at[at], offs_recv.at[at], to)
 
-    def row_of(behind):
-        return pl.ds(lax.rem(y + behind + 8, 8) * 4, 4)
-
     to_partner = offs_copy(pl.ds(b, 1), 0, partner)
-    to_beside = offs_copy(pl.ds(chip * 2, 2), 1, beside)
-    rise = [offs_copy(row_of(-k), 2 + k, up) for k in range(4)]
-    fall = [offs_copy(row_of(k), 6 + k, down) for k in range(3)]
     to_partner.start()
+    to_partner.wait_recv()
+
+    def send_offs(step, carry):
+        offs_copy(pl.ds(chip * 2, 2), 1, along(step)).start()
+        return carry
+
+    lax.fori_loop(1, CHIPS, send_offs, 0)
 
     load_frames.wait()
-    tail.wait_recv()
-
-    @pl.when(t == TILES - 1)
-    def _():
-        ext[pl.ds(ROWS, TAIL), :] = jnp.zeros((TAIL, CH), jnp.bfloat16)
-
-    part = pl.ds(pl.multiple_of(core * HALF, HALF), HALF + TAIL)
-
-    def cols_copy(zt):
-        return remote(ext.at[part], cext, cols_send.at[zt], cols_recv.at[0], (swapped, xl * 8 + zt))
-
-    cols_own = pltpu.make_async_copy(ext.at[part], cext, cols_recv.at[0])
-    for zt in range(8):
-        own = jnp.logical_and(is_own, z == zt)
-
-        @pl.when(jnp.logical_and(is_source, jnp.logical_not(own)))
-        def _():
-            cols_copy(zt).start()
-
-        @pl.when(own)
-        def _():
-            cols_own.start()
-
-    to_partner.wait_recv()
-    to_beside.start()
     load_proj.wait()
     rowsk[0:HALF, :] = sketch_rows(ext[0 : HALF + TAIL, :], proj)
-    to_beside.wait_recv()
-    rise[0].start()
-    fall[0].start()
+    tail.wait_recv()
+
+    @pl.when(t == TILES - 1)
+    def _():
+        ext[pl.ds(ROWS, TAIL), :] = jnp.zeros((TAIL, CH), jnp.bfloat16)
+
+    passes_on = jnp.logical_and(z == 7, y == 0)
+
+    def pass_on(yt):
+        return remote(tail_at, tail_at, pass_send.at[yt], tail_sem.at[1], (b + 4 * yt, t))
+
+    @pl.when(passes_on)
+    def _():
+        for yt in range(1, 8):
+            pass_on(yt).start()
+
     rowsk[HALF:ROWS, :] = sketch_rows(ext[HALF : ROWS + TAIL, :], proj)
-    for k in range(4):
-        rise[k].wait_recv()
-        if k < 3:
-            rise[k + 1].start()
-            fall[k].wait_recv()
-        if k < 2:
-            fall[k + 1].start()
+    every_offs = offs_copy(pl.ds(0, BANDS - 2), 1, along(1))
+    every_offs.wait_recv()
 
     offsets = oall[...]
     reach = offsets + (base + ROWS)
@@ -214,16 +283,21 @@
     load_i.start()
     load_k.start()
 
-    cols_own.wait()
+    sized(lambda rows: cols_own(rows).wait())
+
+    @pl.when(core == 1)
+    def _():
+        next_copy_own.wait()
+
+    @pl.when(jnp.logical_and(core == 1, chunk_block == TILES - 1))
+    def _():
+        cext[pl.ds(HALF, TAIL), :] = jnp.zeros((TAIL, CH), jnp.bfloat16)
+
     colsk[...] = sketch_rows(cext[...], proj)
 
-    low = jnp.full((8, CH), LOW, jnp.float32)
-    table[0] = low
-    whole = low
     for piece in range(PIECES):
         corr_piece(piece, base, colsk, rowsk, xbuf)
-        whole = prefix_piece(piece, whole, xbuf, table)
-    suffix_all(xbuf, table)
+    whole = running_best(xbuf, table)
     load_i.wait()
     load_k.wait()
 
@@ -256,16 +330,21 @@
 
     swap.wait_send()
     every.wait_send()
-    tail.wait_send()
     to_partner.wait_send()
-    to_beside.wait_send()
-    for copy in rise + fall:
-        copy.wait_send()
-    for zt in range(8):
-
-        @pl.when(jnp.logical_and(is_source, jnp.logical_not(jnp.logical_and(is_own, z == zt))))
-        def _():
-            cols_copy(zt).wait_send()
+    every_offs.wait_send()
+
+    @pl.when(gives_tail)
+    def _():
+        tail.wait_send()
+
+    @pl.when(passes_on)
+    def _():
+        for yt in range(1, 8):
+            pass_on(yt).wait_send()
+
+    each_target(
+        lambda zt, rows: cols_copy(zt, rows).wait_send(), lambda zt: next_copy(zt).wait_send(), None, None
+    )
 
 
 def shards(frames, projection, offsets):
@@ -276,10 +355,11 @@
         in_specs=[
             pl.BlockSpec(memory_space=pl.ANY),
             pl.BlockSpec(memory_space=pl.ANY),
-            pl.BlockSpec(memory_space=pltpu.VMEM),
+            pl.BlockSpec(memory_space=pl.ANY),
         ],
         out_specs=pl.BlockSpec(memory_space=pltpu.VMEM),
         scratch_shapes=[
+            pltpu.VMEM((1, NOFF), jnp.int32),
             pltpu.VMEM((ROWS + TAIL, CH), jnp.bfloat16),
             pltpu.VMEM((HALF + TAIL, CH), jnp.bfloat16),
             pltpu.VMEM((TAIL * CH, CH), jnp.bfloat16),
@@ -296,12 +376,14 @@
             pltpu.VMEM((CHIPS, 2, 8, CH), jnp.float32),
             pltpu.VMEM((2, 8, CH), jnp.float32),
             pltpu.VMEM((1, 8, CH), jnp.float32),
-            dma((4,)),
+            dma((5,)),
             dma((2,)),
             dma((8,)),
-            dma((1,)),
-            dma((9,)),
-            dma((9,)),
+            dma((8,)),
+            dma((8,)),
+            dma((2,)),
+            dma((2,)),
+            dma((2,)),
             dma((2,)),
             dma((2,)),
         ],

time: 43.1 us -> 33.4 us (0.77)
  Pallas kernels: 41.7 us -> 32 us
    pallas_call x1, Pallas kernels: 41.7 us -> 32 us  [shards(): pl.pallas_call(kernel, out_shape=jax.ShapeDtypeStruct((1, ROWS), jnp.floa...]
where the time goes in v3:
time: 33.4 us; the launch traced here: 33.2 us
  Pallas kernels  32 us (96%)
  local copies, waits for them, and re-layouts  1.28 us (4%)
    pallas_call x1, Pallas kernels, shards(): pl.pallas_call(kernel, out_shape=jax.ShapeDtypeStruct((1, ROWS), jnp.floa...  32 us
    unnamed x1, local copies, waits for them, and re-layouts  1.28 us

profile of v3, /device:TPU:1, one launch (start us, length us, event | category | flops | bytes accessed | tf_op | source)
XLA Modules:
  0.0 33.2 jit_solution(10611192466680179506)
XLA Ops:
  0.0 32.0 %shard_map.37 = f32[1,1024]{1,0:T(1,128)} custom-call(bf16[1024,128]{1,0:T(8,128)(2,1)} %frames.1, bf16[8192,128]{1,0:T(8,128)(2,1)} %proj_hbm.1, s32[1,8]{1,0:T(1,128)} %offs_hbm.1), custom_call_target="tpu_custom_call" | custom-call | tf_op jit(solution)/shard_map/pallas_call | solution.py:352
  32.0 1.3 %copy.5 = f32[1,1024]{1,0:T(1,128)} copy(f32[1,1024]{1,0:T(1,128)} %shard_map.37) | data formatting | bytes 8192

commit v4 on v3

--- a/solution.py
+++ b/solution.py
@@ -20,6 +20,8 @@
 TILES = 16
 NOFF = 8
 LOW = -256.0
+STEPS = 254
+NONE = -32768
 
 
 def pad_shift(value, by):
@@ -96,28 +98,40 @@
         best = jnp.maximum(best, table[isx[band, n]])
         second = jnp.right_shift(place + ksm[band, n], 10) == 0
         best = jnp.maximum(best, jnp.where(second, whole, LOW))
-    return best * (1.0 / CH)
+    return best
+
+
+def joined_z(y, core):
+    pair = lax.div(y, 2)
+    low = jnp.where(pair == 0, 0, jnp.where(pair == 1, 3, pair - 1))
+    return low + 4 * lax.rem(y + core, 2)
+
+
+def sends_blocks(y, z, core):
+    closes = jnp.logical_and(core == 0, lax.rem(joined_z(y, 1) + 1, 8) == z)
+    return jnp.logical_or(joined_z(y, core) == z, closes)
 
 
 def kernel(
     frames, proj_hbm, offs_hbm, out, offs, ext, cext, proj, rowsk, colsk, xbuf, table, oall, ibuf, kbuf, isx, ksm, sbuf, rbuf,
-    fin, other, local_sem, tail_sem, pass_send, cols_send, next_send, cols_recv, offs_send, offs_recv, out_sem, fin_sem,
+    fin, other, local_sem, tail_sem, pass_send, cols_send, next_send, cols_recv, offs_send, offs_recv, out_sem, fin_sem, ready,
 ):
     b, t = lax.axis_index("band"), lax.axis_index("tile")
     core, xl, y = lax.rem(b, 2), lax.rem(lax.div(b, 2), 2), lax.div(b, 4)
     xh, z = lax.div(t, 8), lax.rem(t, 8)
     chip = lax.div(b, 2)
-    zs = lax.rem(jnp.where(y < 4, 2 * y, 15 - 2 * y) + 4 * core, 8)
+    zs = joined_z(y, core)
     chunk_block = xl * 8 + zs
     base = (t - chunk_block) * ROWS - core * HALF
     partner = (b + 1 - 2 * core, t)
     after, before = lax.rem(t + 1, TILES), lax.rem(t + TILES - 1, TILES)
+    early = z < 4
     is_source = z == zs
-    is_next = jnp.logical_and(lax.rem(before, 8) == zs, core == 1)
     source_own = jnp.logical_and(is_source, xl == xh)
-    next_own = jnp.logical_and(t == lax.rem(chunk_block + 1, TILES), jnp.logical_and(xl == xh, core == 1))
-    next_on_line = lax.div(before, 8) == xl
-    swapped = y * 4 + xh * 2 + core
+    is_next = jnp.logical_and(lax.rem(before, 8) == joined_z(y, 1), core == 0)
+    next_xh = lax.div(before, 8)
+    sends = sends_blocks(y, z, core)
+    other_sends = sends_blocks(y, z, 1 - core)
     gets_tail = jnp.logical_or(z != 7, y == 0)
     gives_tail = jnp.logical_or(z != 0, y == 0)
 
@@ -143,11 +157,11 @@
 
     @pl.when(jnp.logical_not(source_own))
     def _():
-        greet((swapped, chunk_block))
-
-    @pl.when(jnp.logical_and(core == 1, jnp.logical_not(next_own)))
-    def _():
-        greet((swapped, lax.rem(chunk_block + 1, TILES)))
+        greet((y * 4 + xh * 2 + jnp.where(early, core, 1 - core), chunk_block))
+
+    @pl.when(core == 1)
+    def _():
+        greet((y * 4 + xh * 2 + jnp.where(early, 0, 1), lax.rem(chunk_block + 1, TILES)))
 
     @pl.when(gets_tail)
     def _():
@@ -156,7 +170,9 @@
     greet(partner)
 
     def greet_chip(step, carry):
-        greet(along(step))
+        to = lax.rem(chip + step, CHIPS)
+        swapped = sends_blocks(lax.div(to, 2), z, core)
+        greet((to * 2 + jnp.where(swapped, 1 - core, core), t))
         return carry
 
     lax.fori_loop(1, CHIPS, greet_chip, 0)
@@ -164,9 +180,15 @@
     oall[pl.ds(b, 1), :] = jnp.zeros((1, CH), jnp.int32)
     load_offs.wait()
     oall[pl.ds(b, 1), 0:NOFF] = offs[...]
-    as_source = jnp.where(is_source, jnp.where(xl == xh, 7, 8), 0)
-    as_next = jnp.where(is_next, jnp.where(jnp.logical_and(next_on_line, xl == xh), 7, 8), 0)
-    pl.semaphore_wait(barrier, CHIPS + as_source + as_next + jnp.where(gives_tail, 1, 0))
+    def targets(is_one, own, own_here):
+        return jnp.where(is_one, 4 - jnp.where(jnp.logical_and(own, own_here), 1, 0), 0)
+
+    other_source = z == joined_z(y, 1 - core)
+    other_next = jnp.logical_and(lax.rem(before, 8) == joined_z(y, 1), core == 1)
+    as_source = targets(is_source, xl == xh, early) + jnp.where(is_next, 4, 0)
+    as_next = targets(other_source, xl == xh, jnp.logical_not(early)) + jnp.where(other_next, 4, 0)
+    as_band = jnp.where(sends, 0, CHIPS - 1) + jnp.where(other_sends, CHIPS - 1, 0)
+    pl.semaphore_wait(barrier, 1 + as_source + as_next + as_band + jnp.where(gives_tail, 1, 0))
 
     tail_at = ext.at[pl.ds(ROWS, TAIL)]
     tail = remote(frames.at[pl.ds(0, TAIL)], tail_at, tail_sem.at[0], tail_sem.at[1], (b, before))
@@ -177,19 +199,18 @@
 
     def cols_copy(zt, rows):
         part = pl.ds(pl.multiple_of(core * HALF, HALF), rows)
-        return remote(
-            frames.at[part], cext.at[pl.ds(0, rows)], cols_send.at[zt], cols_recv.at[0], (swapped, xl * 8 + zt)
-        )
+        to = (y * 4 + xh * 2 + core, xl * 8 + zt)
+        return remote(frames.at[part], cext.at[pl.ds(0, rows)], cols_send.at[zt], cols_recv.at[0], to)
 
     def cols_own(rows):
         part = pl.ds(pl.multiple_of(core * HALF, HALF), rows)
         return pltpu.make_async_copy(frames.at[part], cext.at[pl.ds(0, rows)], cols_recv.at[0])
 
+    close_at = cext.at[pl.ds(HALF, TAIL)]
+
     def next_copy(zt):
-        to = (y * 4 + lax.div(before, 8) * 2 + core, xl * 8 + zt)
-        return remote(frames.at[pl.ds(0, TAIL)], cext.at[pl.ds(HALF, TAIL)], next_send.at[zt], cols_recv.at[1], to)
-
-    next_copy_own = pltpu.make_async_copy(frames.at[pl.ds(0, TAIL)], cext.at[pl.ds(HALF, TAIL)], cols_recv.at[1])
+        to = (y * 4 + next_xh * 2 + 1, xl * 8 + zt)
+        return remote(frames.at[pl.ds(0, TAIL)], close_at, next_send.at[zt], cols_recv.at[1], to)
 
     def sized(what):
         @pl.when(core == 0)
@@ -200,10 +221,15 @@
         def _():
             what(HALF)
 
-    def each_target(cols_do, next_do, cols_do_own, next_do_own):
+    def each_target(zts, cols_do, next_do, cols_do_own):
+        @pl.when(is_next)
+        def _():
+            for zt in zts:
+                next_do(zt)
+
         @pl.when(is_source)
         def _():
-            for zt in range(8):
+            for zt in zts:
                 own = jnp.logical_and(source_own, z == zt)
 
                 @pl.when(jnp.logical_not(own))
@@ -216,27 +242,25 @@
                     def _():
                         sized(cols_do_own)
 
-        @pl.when(is_next)
-        def _():
-            for zt in range(8):
-                own = jnp.logical_and(next_own, z == zt)
-
-                @pl.when(jnp.logical_not(own))
-                def _():
-                    next_do(zt)
-
-                if next_do_own is not None:
-
-                    @pl.when(own)
-                    def _():
-                        next_do_own()
-
-    each_target(
-        lambda zt, rows: cols_copy(zt, rows).start(),
-        lambda zt: next_copy(zt).start(),
-        lambda rows: cols_own(rows).start(),
-        lambda: next_copy_own.start(),
-    )
+    def start_to(zts):
+        each_target(
+            zts,
+            lambda zt, rows: cols_copy(zt, rows).start(),
+            lambda zt: next_copy(zt).start(),
+            lambda rows: cols_own(rows).start(),
+        )
+
+    start_to(range(4))
+
+    @pl.when(other_sends)
+    def _():
+        pl.semaphore_signal(ready, inc=1, device_id=partner, device_id_type=MESH)
+
+    @pl.when(sends)
+    def _():
+        pl.semaphore_wait(ready, 1)
+
+    start_to(range(4, 8))
 
     def offs_copy(rows, at, to):
         return remote(oall.at[rows], oall.at[rows], offs_send.at[at], offs_recv.at[at], to)
@@ -271,6 +295,20 @@
             pass_on(yt).start()
 
     rowsk[HALF:ROWS, :] = sketch_rows(ext[HALF : ROWS + TAIL, :], proj)
+    sized(lambda rows: cols_own(rows).wait())
+
+    @pl.when(core == 1)
+    def _():
+        pltpu.make_async_copy(frames.at[pl.ds(0, TAIL)], close_at, cols_recv.at[1]).wait()
+
+    @pl.when(jnp.logical_and(core == 1, chunk_block == TILES - 1))
+    def _():
+        cext[pl.ds(HALF, TAIL), :] = jnp.zeros((TAIL, CH), jnp.bfloat16)
+
+    colsk[...] = sketch_rows(cext[...], proj)
+
+    for piece in range(PIECES):
+        corr_piece(piece, base, colsk, rowsk, xbuf)
     every_offs = offs_copy(pl.ds(0, BANDS - 2), 1, along(1))
     every_offs.wait_recv()
 
@@ -283,20 +321,6 @@
     load_i.start()
     load_k.start()
 
-    sized(lambda rows: cols_own(rows).wait())
-
-    @pl.when(core == 1)
-    def _():
-        next_copy_own.wait()
-
-    @pl.when(jnp.logical_and(core == 1, chunk_block == TILES - 1))
-    def _():
-        cext[pl.ds(HALF, TAIL), :] = jnp.zeros((TAIL, CH), jnp.bfloat16)
-
-    colsk[...] = sketch_rows(cext[...], proj)
-
-    for piece in range(PIECES):
-        corr_piece(piece, base, colsk, rowsk, xbuf)
     whole = running_best(xbuf, table)
     load_i.wait()
     load_k.wait()
@@ -306,25 +330,33 @@
     def out_copy(src, dst, to):
         return remote(sbuf.at[src], rbuf.at[dst], out_sem.at[0], out_sem.at[1], (to * 2 + core, t))
 
+    def coded(to):
+        both = [band_best(to * 2 + side, isx, ksm, table, whole, place) for side in range(2)]
+        scaled = jnp.maximum(jnp.concatenate(both, axis=0) * STEPS, NONE)
+        return jnp.round(scaled).astype(jnp.int32).astype(jnp.int16)
+
     def send_best(k, carry):
         step = 8 + jnp.where(lax.rem(k, 2) == 1, lax.div(k + 1, 2), -lax.div(k, 2))
         to = lax.rem(chip + step, CHIPS)
-        for side in range(2):
-            sbuf[to, side] = band_best(to * 2 + side, isx, ksm, table, whole, place)
+        sbuf[to] = coded(to)
         out_copy(pl.ds(to, 1), pl.ds(chip, 1), to).start()
         return carry
 
     lax.fori_loop(0, CHIPS - 1, send_best, 0)
-    for side in range(2):
-        rbuf[chip, side] = band_best(chip * 2 + side, isx, ksm, table, whole, place)
+    rbuf[chip] = coded(chip)
 
     every = out_copy(pl.ds(0, CHIPS - 1), pl.ds(0, CHIPS - 1), chip)
     every.wait_recv()
-    fin[...] = jnp.max(rbuf[...], axis=0)
+    top = rbuf[0].astype(jnp.int32)
+    for k in range(1, CHIPS):
+        top = jnp.maximum(top, rbuf[k].astype(jnp.int32))
+    fin[0] = top[0:8]
+    fin[1] = top[8:16]
     swap = remote(fin.at[pl.ds(1 - core, 1)], other, fin_sem.at[0], fin_sem.at[1], partner)
     swap.start()
     swap.wait_recv()
-    best = jnp.maximum(fin[core], other[0])
+    code = jnp.maximum(fin[core], other[0])
+    best = jnp.where(code == NONE, -2.0, code.astype(jnp.float32) * (1.0 / (STEPS * CH)))
     for group in range(8):
         out[:, CH * group : CH * (group + 1)] = best[group : group + 1, :]
 
@@ -342,9 +374,7 @@
         for yt in range(1, 8):
             pass_on(yt).wait_send()
 
-    each_target(
-        lambda zt, rows: cols_copy(zt, rows).wait_send(), lambda zt: next_copy(zt).wait_send(), None, None
-    )
+    each_target(range(8), lambda zt, rows: cols_copy(zt, rows).wait_send(), lambda zt: next_copy(zt).wait_send(), None)
 
 
 def shards(frames, projection, offsets):
@@ -372,10 +402,10 @@
             pltpu.VMEM((BANDS, CH), jnp.int32),
             pltpu.SMEM((BANDS, CH), jnp.int32),
             pltpu.SMEM((BANDS, CH), jnp.int32),
-            pltpu.VMEM((CHIPS, 2, 8, CH), jnp.float32),
-            pltpu.VMEM((CHIPS, 2, 8, CH), jnp.float32),
-            pltpu.VMEM((2, 8, CH), jnp.float32),
-            pltpu.VMEM((1, 8, CH), jnp.float32),
+            pltpu.VMEM((CHIPS, 16, CH), jnp.int16),
+            pltpu.VMEM((CHIPS, 16, CH), jnp.int16),
+            pltpu.VMEM((2, 8, CH), jnp.int32),
+            pltpu.VMEM((1, 8, CH), jnp.int32),
             dma((5,)),
             dma((2,)),
             dma((8,)),
@@ -386,6 +416,7 @@
             dma((2,)),
             dma((2,)),
             dma((2,)),
+            pltpu.SemaphoreType.REGULAR,
         ],
         compiler_params=pltpu.CompilerParams(
             collective_id=0, has_side_effects=True, vmem_limit_bytes=62 * 1024 * 1024

time: 33.4 us -> 31 us (0.928)
  Pallas kernels: 32 us -> 29.5 us
    pallas_call x1, Pallas kernels: 32 us -> 29.5 us  [shards(): pl.pallas_call(kernel, out_shape=jax.ShapeDtypeStruct((1, ROWS), jnp.floa...]
where the time goes in v4:
time: 31 us; the launch traced here: 30.8 us
  Pallas kernels  29.5 us (95%)
  local copies, waits for them, and re-layouts  1.28 us (4%)
    pallas_call x1, Pallas kernels, shards(): pl.pallas_call(kernel, out_shape=jax.ShapeDtypeStruct((1, ROWS), jnp.floa...  29.5 us
    unnamed x1, local copies, waits for them, and re-layouts  1.28 us

profile of v4, /device:TPU:1, one launch (start us, length us, event | category | flops | bytes accessed | tf_op | source)
XLA Modules:
  0.0 30.8 jit_solution(1977205109976831058)
XLA Ops:
  0.0 29.5 %shard_map.37 = f32[1,1024]{1,0:T(1,128)} custom-call(bf16[1024,128]{1,0:T(8,128)(2,1)} %frames.1, bf16[8192,128]{1,0:T(8,128)(2,1)} %proj_hbm.1, s32[1,8]{1,0:T(1,128)} %offs_hbm.1), custom_call_target="tpu_custom_call" | custom-call | tf_op jit(solution)/shard_map/pallas_call | solution.py:382
  29.5 1.3 %copy.5 = f32[1,1024]{1,0:T(1,128)} copy(f32[1,1024]{1,0:T(1,128)} %shard_map.37) | data formatting | bytes 8192

commit v5 on v4

--- a/solution.py
+++ b/solution.py
@@ -19,6 +19,7 @@
 CHIPS = 16
 TILES = 16
 NOFF = 8
+GRANT = (54 * 1024 - 128) * 1024
 LOW = -256.0
 STEPS = 254
 NONE = -32768
@@ -113,7 +114,7 @@
 
 
 def kernel(
-    frames, proj_hbm, offs_hbm, out, offs, ext, cext, proj, rowsk, colsk, xbuf, table, oall, ibuf, kbuf, isx, ksm, sbuf, rbuf,
+    frames, proj_hbm, offs, out, ext, cext, proj, rowsk, colsk, xbuf, table, oall, ibuf, kbuf, isx, ksm, sbuf, rbuf,
     fin, other, local_sem, tail_sem, pass_send, cols_send, next_send, cols_recv, offs_send, offs_recv, out_sem, fin_sem, ready,
 ):
     b, t = lax.axis_index("band"), lax.axis_index("tile")
@@ -141,8 +142,6 @@
         )
 
     load_frames = pltpu.make_async_copy(frames, ext.at[pl.ds(0, ROWS)], local_sem.at[0])
-    load_offs = pltpu.make_async_copy(offs_hbm, offs, local_sem.at[4])
-    load_offs.start()
     load_frames.start()
     load_proj = pltpu.make_async_copy(proj_hbm, proj, local_sem.at[1])
     load_proj.start()
@@ -178,7 +177,6 @@
     lax.fori_loop(1, CHIPS, greet_chip, 0)
 
     oall[pl.ds(b, 1), :] = jnp.zeros((1, CH), jnp.int32)
-    load_offs.wait()
     oall[pl.ds(b, 1), 0:NOFF] = offs[...]
     def targets(is_one, own, own_here):
         return jnp.where(is_one, 4 - jnp.where(jnp.logical_and(own, own_here), 1, 0), 0)
@@ -385,11 +383,10 @@
         in_specs=[
             pl.BlockSpec(memory_space=pl.ANY),
             pl.BlockSpec(memory_space=pl.ANY),
-            pl.BlockSpec(memory_space=pl.ANY),
+            pl.BlockSpec(memory_space=pltpu.VMEM),
         ],
         out_specs=pl.BlockSpec(memory_space=pltpu.VMEM),
         scratch_shapes=[
-            pltpu.VMEM((1, NOFF), jnp.int32),
             pltpu.VMEM((ROWS + TAIL, CH), jnp.bfloat16),
             pltpu.VMEM((HALF + TAIL, CH), jnp.bfloat16),
             pltpu.VMEM((TAIL * CH, CH), jnp.bfloat16),
@@ -406,7 +403,7 @@
             pltpu.VMEM((CHIPS, 16, CH), jnp.int16),
             pltpu.VMEM((2, 8, CH), jnp.int32),
             pltpu.VMEM((1, 8, CH), jnp.int32),
-            dma((5,)),
+            dma((4,)),
             dma((2,)),
             dma((8,)),
             dma((8,)),
@@ -419,7 +416,7 @@
             pltpu.SemaphoreType.REGULAR,
         ],
         compiler_params=pltpu.CompilerParams(
-            collective_id=0, has_side_effects=True, vmem_limit_bytes=62 * 1024 * 1024
+            collective_id=0, has_side_effects=True, vmem_limit_bytes=GRANT
         ),
     )(frames, projection, offsets)
 

time: 31 us -> 30.3 us (0.977)
  Pallas kernels: 29.5 us -> 28.9 us
    pallas_call x1, Pallas kernels: 29.5 us -> 28.9 us  [shards(): pl.pallas_call(kernel, out_shape=jax.ShapeDtypeStruct((1, ROWS), jnp.floa...]
    unnamed x1 -> x3, local copies, waits for them, and re-layouts: 1.28 us -> 1.25 us
where the time goes in v5:
time: 30.3 us; the launch traced here: 30.2 us
  Pallas kernels  28.9 us (95%)
  local copies, waits for them, and re-layouts  1.25 us (4%)
    pallas_call x1, Pallas kernels, shards(): pl.pallas_call(kernel, out_shape=jax.ShapeDtypeStruct((1, ROWS), jnp.floa...  28.9 us
    unnamed x3, local copies, waits for them, and re-layouts  1.25 us

profile of v5, /device:TPU:1, one launch (start us, length us, event | category | flops | bytes accessed | tf_op | source)
XLA Modules:
  0.0 30.2 jit_solution(18398479297338328598)
XLA Ops:
  0.0 0.0 copy-start
  0.0 0.7 %copy-done = s32[1,8]{1,0:T(1,128)S(1)} copy-done((s32[1,8]{1,0:T(1,128)S(1)}, s32[1,8]{1,0:T(1,128)}, u32[]{:S(2)}) %copy-start) | copy-done | bytes 56
  0.7 28.9 %shard_map.37 = f32[1,1024]{1,0:T(1,128)S(1)} custom-call(bf16[1024,128]{1,0:T(8,128)(2,1)} %frames.1, bf16[8192,128]{1,0:T(8,128)(2,1)} %proj_hbm.1, s32[1,8]{1,0:T(1,128)S(1)} %copy-done), custom_call_target="tpu_custom_call" | custom-call | tf_op jit(solution)/shard_map/pallas_call | solution.py:380
  29.6 0.6 %copy.5 = f32[1,1024]{1,0:T(1,128)} copy(f32[1,1024]{1,0:T(1,128)S(1)} %shard_map.37) | data formatting | bytes 8192
Async XLA Ops:
  0.0 0.7 %copy-start = (s32[1,8]{1,0:T(1,128)S(1)}, s32[1,8]{1,0:T(1,128)}, u32[]{:S(2)}) copy-start(s32[1,8]{1,0:T(1,128)} %offs.1) | copy-start | bytes 100
